TPU v7x, 32 devices: a whole 2x2x4 slice. The times are simulated.
32 devices in a mesh: gx: 4 (over y, x), gy: 8 (over z, core).
Axes of the slice: x: 2, y: 2, z: 4, core: 2. Of those that a mesh axis runs over, the one named last changes fastest.
Arguments:
- energy: float32 [64, 1024, 128], P('gx', 'gy'), may hold values from 1 to 5
- coupling: float32 [64, 1024, 128], P('gx', 'gy'), may hold values from 4000 to 40000
Outputs:
- energy_next: float32 [64, 1024, 128], P('gx', 'gy')
All inputs are finite; a program needn't handle non-finite values.
Results may differ from a plain program's by a relative error of at most 0.0003.
Values sent between devices are 32-bit elements; how exact they have to be, the bound alone decides.
A program may use at most 64 MiB of HBM per device.

v0:
```python
import jax
import jax.numpy as jnp
from jax import lax
from jax.sharding import PartitionSpec as P

y_weight = 0.15


def with_halo(shard, sides, width):
    for axis, dim in sides:
        size, length = (lax.axis_size(axis), shard.shape[dim])
        up = [(i, (i + 1) % size) for i in range(size - 1)]
        down = [(j, i) for i, j in up]
        last = lax.slice_in_dim(shard, length - width, length, axis=dim)
        initial = lax.slice_in_dim(shard, 0, width, axis=dim)
        before = lax.ppermute(last, axis, up)
        after = lax.ppermute(initial, axis, down)
        shard = jnp.concatenate([before, shard, after], axis=dim)
    return shard


def shifted(value, axis, steps):
    count = lax.axis_size(axis)
    initial, last = (max(0, -steps), min(count, count - steps))
    return lax.ppermute(value, axis, [(source, source + steps) for source in range(initial, last)])


def many_solve(diag_part, lower_part, upper_part, sources):

    def forward(running, row):
        prev_ratio, prev_value = running
        diag_row, lower_row, upper_row, source_row = row
        denom = diag_row - lower_row * prev_ratio
        new_ratio = upper_row / denom
        new_value = (source_row - lower_row[None] * prev_value) / denom[None]
        return ((new_ratio, new_value), (new_ratio, new_value))

    start = (jnp.zeros(diag_part.shape[1:], jnp.float32), jnp.zeros(sources.shape[1:], jnp.float32))
    _, (ratios, values) = lax.scan(forward, start, (diag_part, lower_part, upper_part, sources))

    def backward(later_value, row):
        ratio_row, value_row = row
        result = value_row - ratio_row[None] * later_value
        return (result, result)

    _, solved = lax.scan(
        backward, jnp.zeros(sources.shape[1:], jnp.float32), (ratios, values), reverse=True
    )
    return solved


def body(energy, coupling):
    padded = with_halo(energy, (("gy", 1),), 1)
    source_term = energy + y_weight * (padded[:, :-2] - 2.0 * energy + padded[:, 2:])
    height = energy.shape[0]
    inner_diag = 1.0 + coupling[: height - 1] + coupling[1:height]
    inner_lower = -coupling[: height - 1]
    inner_upper = -coupling[1:height]
    blank = jnp.zeros_like(coupling[: height - 1])
    left_source = jnp.concatenate([coupling[:1], blank[1:]], 0)
    right_source = jnp.concatenate([blank[1:], coupling[height - 1 : height]], 0)
    sources = jnp.stack([source_term[: height - 1], left_source, right_source], 1)
    solved = many_solve(inner_diag, inner_lower, inner_upper, sources)
    local_part = solved[:, 0]
    left_reply = solved[:, 1]
    right_reply = solved[:, 2]
    first_rows = jnp.stack([local_part[0], left_reply[0], right_reply[0], coupling[0]], 0)
    following = shifted(first_rows, "gx", -1)
    next_local = following[0]
    next_left = following[1]
    next_right = following[2]
    next_face = following[3]
    own_face = coupling[height - 1]
    position = lax.axis_index("gx")
    lower_coef = jnp.where(position == 0, 0.0, -own_face * left_reply[height - 2])
    middle = 1.0 + own_face + next_face - own_face * right_reply[height - 2] - next_face * next_left
    upper_coef = -next_face * next_right
    target = source_term[height - 1] + own_face * local_part[height - 2] + next_face * next_local
    bundle = jnp.stack([lower_coef, middle, upper_coef, target], 0)[None]
    gathered = lax.all_gather(bundle, "gx", axis=0, tiled=True)
    whole = many_solve(gathered[:, 1], gathered[:, 0], gathered[:, 2], gathered[:, 3][:, None])
    last_value = lax.dynamic_index_in_dim(whole[:, 0], position, 0, keepdims=False)
    previous = shifted(last_value, "gx", 1)
    interior = local_part + left_reply * previous[None] + right_reply * last_value[None]
    return jnp.concatenate([interior, last_value[None]], 0)


def solution(mesh):
    in_specs = (P("gx", "gy", None), P("gx", "gy", None))
    out_specs = P("gx", "gy", None)
    return jax.shard_map(body, mesh=mesh, in_specs=in_specs, out_specs=out_specs, check_vma=False)
```

profile of v0, /device:TPU:0, one launch (start us, length us, event | category | flops | bytes accessed | tf_op | source)
XLA Modules:
  0.0 161.7 jit_solution(15432872547918712840)
XLA Ops:
  7.4 2.4 %collective-permute-start = (f32[16,1,128]{2,1,0:T(1,128)S(1)}, f32[16,1,128]{2,1,0:T(1,128)S(1)}, u32[]{:S(2)}, u32[]{:S(2)}) collective-permute-start(f32[16,1,128]{2,1,0:T(1,128)S(1)} %get-tuple-element.507), channel_id=1, source_target_pairs={{0,1},{1,2},{2,3},{3,4},{4,5},{5,6},{6,7},{8,9},{9,10},{10,11},{11... | collective-permute-start | bytes 24584 | tf_op jit(solution)/shard_map/ppermute | solution.py:16
  9.8 1.3 collective-permute-start.1
  12.0 3.7 %select_bitcast_fusion = (f32[15,1,128,128]{3,2,0,1:T(8,128)}, f32[15,128,128]{2,1,0:T(8,128)}, f32[15,128,128]{2,1,0:T(8,128)}, f32[15,128,128]{2,1,0:T(8,128)}) fusion(f32[16,128,128]{2,1,0:T(8,128)} %param.11, pred[15]{0:T(512)(128)(4,1)} %constant.131.clone.1), kind=kLoop, calls=%fused_computation.41 | loop fusion | flops 1228800 | bytes 5898255 | tf_op jit(solution)/shard_map/stack | solution.py:62
  15.7 1.1 pad_bitcast_fusion
  18.9 1.9 %broadcast.28.clone = f32[15,3,128,128]{3,2,1,0:T(8,128)} broadcast(f32[]{:T(128)} %constant.127.clone.1), dimensions={} | broadcast | bytes 2949124 | tf_op jit(solution)/shard_map/broadcast.8
  20.8 1.1 broadcast_in_dim.56
  21.9 34.4 %while.68 = (s32[]{:T(128)}, f32[128,128]{1,0:T(8,128)S(1)}, f32[3,128,128]{2,1,0:T(8,128)S(1)}, f32[15,128,128]{2,1,0:T(8,128)}, f32[15,3,128,128]{3,2,1,0:T(8,...) while((s32[]{:T(128)}, f32[128,128]{1,0:T(8,128)S(1)}, ...), condition=%wide.region_1.2_spmd.clone, body=%wide.region_0.1_spmd.clone.sunk | while | flops 262147 | bytes 1442936 | solution.py:39
  21.9 1.5 bitcast_dynamic-update-slice_fusion.12
  24.2 1.5 bitcast_dynamic-update-slice_fusion.12
  26.4 1.5 bitcast_dynamic-update-slice_fusion.12
  28.7 1.5 bitcast_dynamic-update-slice_fusion.12
  31.0 1.5 bitcast_dynamic-update-slice_fusion.12
  33.3 1.5 bitcast_dynamic-update-slice_fusion.12
  35.6 1.5 bitcast_dynamic-update-slice_fusion.12
  37.9 1.5 bitcast_dynamic-update-slice_fusion.12
  40.2 1.5 bitcast_dynamic-update-slice_fusion.12
  42.5 1.5 bitcast_dynamic-update-slice_fusion.12
  44.8 1.5 bitcast_dynamic-update-slice_fusion.12
  47.1 1.5 bitcast_dynamic-update-slice_fusion.12
  49.3 1.5 bitcast_dynamic-update-slice_fusion.12
  51.6 1.5 bitcast_dynamic-update-slice_fusion.12
  53.9 1.5 bitcast_dynamic-update-slice_fusion.12
  56.6 28.5 %while.69 = (s32[]{:T(128)}, f32[3,128,128]{2,1,0:T(8,128)S(1)}, f32[15,3,128,128]{3,2,1,0:T(8,128)S(1)}, f32[15,3,128,128]{3,2,1,0:T(8,128)}, f32[15,128,128]{2...) while((s32[]{:T(128)}, f32[3,128,128]{2,1,0:T(8,128)S(1)}, f32[15,3,128,128]{3,2,1,0:T(8,128)S(1)}, ...), condition=%wide.region_3.4_spmd.clone, body=%wide.region_2.3_spmd.clone.sunk | while | flops 147460 | bytes 983155 | solution.py:46
  57.4 1.0 bitcast_dynamic-update-slice_fusion.14
  61.2 1.0 bitcast_dynamic-update-slice_fusion.14
  63.1 1.0 bitcast_dynamic-update-slice_fusion.14
  65.0 1.0 bitcast_dynamic-update-slice_fusion.14
  85.2 1.3 collective-permute-start.2
  86.5 8.0 %collective-permute-done.2 = f32[4,128,128]{2,1,0:T(8,128)S(1)} collective-permute-done((f32[4,128,128]{2,1,0:T(8,128)S(1)}, f32[4,128,128]{2,1,0:T(8,128)S(1)}, u32[]{:S(2)}, u32[]{:S(2)}) %collective-permute-start.2) | collective-permute-done | bytes 262176 | tf_op jit(solution)/shard_map/ppermute | solution.py:25
  96.1 31.1 %all-gather.3.cloned.1.call-done = f32[16,128,128]{2,1,0:T(8,128)} async-done(((f32[4,128,128]{2,1,0:T(8,128)}), f32[16,128,128]{2,1,0:T(8,128)}) %all-gather.3.cloned.1.call-update) | async-done | bytes 1048592 | tf_op jit(solution)/shard_map/all_gather | solution.py:80
  127.2 2.1 %fusion.15 = (f32[4,1,128,128]{3,2,1,0:T(8,128)}, f32[4,128,128]{2,1,0:T(8,128)S(1)}, f32[4,128,128]{2,1,0:T(8,128)S(1)}, f32[4,128,128]{2,1,0:T(8,128)}) fusion(f32[4,4,128,128]{3,2,1,0:T(8,128)} %bitcast.136), kind=kLoop, calls=%fused_computation.66 | loop fusion | bytes 2097152 | tf_op jit(solution)/shard_map/slice | solution.py:81
  130.0 12.1 %while.70 = (s32[]{:T(128)}, f32[128,128]{1,0:T(8,128)S(1)}, f32[1,128,128]{2,1,0:T(8,128)}, f32[4,128,128]{2,1,0:T(8,128)}, f32[4,1,128,128]{3,2,1,0:T(8,128)},...) while((s32[]{:T(128)}, f32[128,128]{1,0:T(8,128)S(1)}, ...), condition=%wide.region_5.6_spmd.clone, body=%wide.region_4.5_spmd.clone.sunk | while | flops 180227 | bytes 854135 | solution.py:39
  130.0 1.5 bitcast_dynamic-update-slice_fusion.16
  131.5 1.5 bitcast_dynamic-update-slice_fusion.15
  133.0 1.6 bitcast_dynamic-update-slice_fusion.16
  134.6 1.5 bitcast_dynamic-update-slice_fusion.15
  136.0 1.6 bitcast_dynamic-update-slice_fusion.16
  137.6 1.5 bitcast_dynamic-update-slice_fusion.15
  139.1 1.5 bitcast_dynamic-update-slice_fusion.16
  140.6 1.5 bitcast_dynamic-update-slice_fusion.15
  142.2 6.1 %while.71 = (s32[]{:T(128)}, f32[1,128,128]{2,1,0:T(8,128)}, f32[4,1,128,128]{3,2,1,0:T(8,128)S(1)}, f32[4,1,128,128]{3,2,1,0:T(8,128)}, f32[4,128,128]{2,1,0:T(8,128)}, /*index=5*/s32[]{:T(128)}, s32[]{:T(128)}, s32[]{:T(128)}) while((s32[]{:T(128)}, f32[1,128,128]{2,1,0:T(8,128)}, f32[4,1,128,128]{3,2,1,0:T(8,128)S(1)}, ...), condition=%wide.region_7.8_spmd.clone, body=%wide.region_6.7_spmd.clone.sunk | while | flops 49156 | bytes 327791 | solution.py:46
  142.2 1.5 bitcast_dynamic-update-slice_fusion.17
  143.7 1.5 bitcast_dynamic-update-slice_fusion.17
  145.2 1.5 bitcast_dynamic-update-slice_fusion.17
  146.8 1.5 bitcast_dynamic-update-slice_fusion.17
  148.3 3.4 %collective-permute-start.3 = (f32[128,128]{1,0:T(8,128)S(1)}, f32[128,128]{1,0:T(8,128)S(1)}, u32[]{:S(2)}, u32[]{:S(2)}) collective-permute-start(f32[128,128]{1,0:T(8,128)S(1)} %get-tuple-element.516), channel_id=1, source_target_pairs={{0,8},{8,16},{16,24},{1,9},{9,17},{17,25},{2,10},{10,18},{18,26},{... | collective-permute-start | bytes 196616 | tf_op jit(solution)/shard_map/ppermute | solution.py:25
  151.7 1.9 %collective-permute-done.3 = f32[128,128]{1,0:T(8,128)S(1)} collective-permute-done((f32[128,128]{1,0:T(8,128)S(1)}, f32[128,128]{1,0:T(8,128)S(1)}, u32[]{:S(2)}, u32[]{:S(2)}) %collective-permute-start.3) | collective-permute-done | bytes 65568 | tf_op jit(solution)/shard_map/ppermute | solution.py:25
  153.8 1.0 pad_maximum_fusion.3
  (74 shorter events, 42.1 us)
Async XLA Ops:
  6.5 120.7 %all-gather.3.cloned.1.call-start = ((), (), s32[]{:S(2)}) async-start(), calls=%async_computation | async-start | bytes 1310720 | tf_op jit(solution)/shard_map/all_gather | solution.py:80
  7.4 9.4 %collective-permute-start = (f32[16,1,128]{2,1,0:T(1,128)S(1)}, f32[16,1,128]{2,1,0:T(1,128)S(1)}, u32[]{:S(2)}, u32[]{:S(2)}) collective-permute-start(f32[16,1,128]{2,1,0:T(1,128)S(1)} %get-tuple-element.507), channel_id=1, source_target_pairs={{0,1},{1,2},{2,3},{3,4},{4,5},{5,6},{6,7},{8,9},{9,10},{10,11},{11... | collective-permute-start | bytes 24584 | tf_op jit(solution)/shard_map/ppermute | solution.py:16
  9.8 7.0 %collective-permute-start.1 = (f32[16,1,128]{2,1,0:T(1,128)S(1)}, f32[16,1,128]{2,1,0:T(1,128)S(1)}, u32[]{:S(2)}, u32[]{:S(2)}) collective-permute-start(f32[16,1,128]{2,1,0:T(1,128)S(1)} %get-tuple-element.508), channel_id=1, source_target_pairs={{1,0},{2,1},{3,2},{4,3},{5,4},{6,5},{7,6},{9,8},{10,9},{11,10},{12... | collective-permute-start | bytes 24584 | tf_op jit(solution)/shard_map/ppermute | solution.py:17
  12.0 4.8 %copy-start.3 = (f32[16,128,128]{2,1,0:T(8,128)S(1)}, f32[16,128,128]{2,1,0:T(8,128)}, u32[]{:S(2)}) copy-start(f32[16,128,128]{2,1,0:T(8,128)} %param.10) | copy-start | bytes 3145732
  16.8 1.3 copy-start.1
  16.8 1.9 %copy-start.2 = (f32[15,1,128,128]{3,2,0,1:T(8,128)S(1)}, f32[15,1,128,128]{3,2,0,1:T(8,128)}, u32[]{:S(2)}) copy-start(f32[15,1,128,128]{3,2,0,1:T(8,128)} %pad_bitcast_fusion) | copy-start | bytes 2949124
  17.1 1.0 copy-start
  85.2 9.3 %collective-permute-start.2 = (f32[4,128,128]{2,1,0:T(8,128)S(1)}, f32[4,128,128]{2,1,0:T(8,128)S(1)}, u32[]{:S(2)}, u32[]{:S(2)}) collective-permute-start(f32[4,128,128]{2,1,0:T(8,128)S(1)} %pad_maximum_fusion.4), channel_id=1, source_target_pairs={{8,0},{16,8},{24,16},{9,1},{17,9},{25,17},{10,2},{18,10},{26,18},{... | collective-permute-start | bytes 786440 | tf_op jit(solution)/shard_map/ppermute | solution.py:25
  148.3 5.3 %collective-permute-start.3 = (f32[128,128]{1,0:T(8,128)S(1)}, f32[128,128]{1,0:T(8,128)S(1)}, u32[]{:S(2)}, u32[]{:S(2)}) collective-permute-start(f32[128,128]{1,0:T(8,128)S(1)} %get-tuple-element.516), channel_id=1, source_target_pairs={{0,8},{8,16},{16,24},{1,9},{9,17},{17,25},{2,10},{10,18},{18,26},{... | collective-permute-start | bytes 196616 | tf_op jit(solution)/shard_map/ppermute | solution.py:25
Sparse Core Ops, SparseCore 0:
  96.2 30.9 all-gather.2
where the time goes:
time: 165 us; the launch traced here: 162 us
  other arithmetic  75.3 us (46%)
  waiting for transfers between devices  40.9 us (25%)
  local copies, waits for them, and re-layouts  23.2 us (14%)
  between operations  13.6 us (8%)
  starting transfers between devices  8.3 us (5%)
    dynamic_update_slice x57, other arithmetic, many_solve(): lax.scan(forward, start, (diag_part, lower_part, upper_part, sources))  68.2 us
    all_gather x1, waiting for transfers between devices, body(): gathered = lax.all_gather(bundle, 'gx', axis=0, tiled=True)  31.1 us
    mul x15, local copies, waits for them, and re-layouts, backward(): result = value_row - ratio_row[None] * later_value  12.7 us
    ppermute x2, waiting for transfers between devices, shifted(): lax.ppermute(value, axis, [(source, source + steps) for source in range(i...  9.85 us
    ppermute x2, starting transfers between devices, shifted(): lax.ppermute(value, axis, [(source, source + steps) for source in range(i...  4.65 us
    another operation x2, other arithmetic, body(): jnp.stack([source_term[:height - 1], left_source, right_source], 1)  3.92 us
  transfers between devices with their start and end apart: 5, of which 3 were waited for; matrix products, arithmetic and copies ran while one was open for 4% of the time, Pallas kernels for 0%

commit v1 on v0

v1 whole, which is shorter than its diff:
```python
import functools

import jax
import jax.numpy as jnp
from jax import lax
from jax.experimental import pallas as pl
from jax.experimental.pallas import tpu as pltpu
from jax.sharding import PartitionSpec as P

Y_WEIGHT = 0.15
CHUNKS = 4
LAG = 2
PAD = 8
MESH = pl.DeviceIdType.MESH


def kernel(
    gx_size, gy_size, chunks, lag,
    energy_ref, coupling_ref, out_ref,
    e_v, c_v, b_v, r_v, g_v, edge, halo, outbox, inbox, usend, ubox,
    load_sem, face_sem, halo_send, halo_recv, msg_send, msg_recv, u_send, u_recv,
):
    height, width, _ = energy_ref.shape
    size = width // chunks
    p, q = lax.axis_index("gx"), lax.axis_index("gy")
    half = gx_size // 2
    is_left = p < half
    is_right = p >= half
    is_end = (p == 0) | (p == gx_size - 1)
    is_mid = (p == half - 1) | (p == half)
    not_end = jnp.logical_not(is_end)
    not_mid = jnp.logical_not(is_mid)
    inward = jnp.where(is_left, p + 1, p - 1)
    outward = jnp.where(is_left, p - 1, p + 1)
    slot = jnp.where(is_mid, 1, 0)
    order = list(range(1, chunks - 1)) + [0, chunks - 1] if chunks > 2 else list(range(chunks))

    barrier = pltpu.get_barrier_semaphore()
    has_down, has_up = q > 0, q < gy_size - 1

    def greet(cond, device):
        @pl.when(cond)
        def _():
            pl.semaphore_signal(barrier, inc=1, device_id=device, device_id_type=MESH)

    greet(p > 0, (p - 1, q))
    greet(p < gx_size - 1, (p + 1, q))
    greet(has_down, (p, q - 1))
    greet(has_up, (p, q + 1))

    load = pltpu.make_async_copy(energy_ref, e_v.at[:, PAD:PAD + width, :], load_sem)
    load.start()

    def face_load(k):
        cut = pl.ds(k * size, size)
        return pltpu.make_async_copy(coupling_ref.at[:, cut, :], c_v.at[:, cut, :], face_sem.at[k])

    for k in order:
        face_load(k).start()

    @pl.when(is_end)
    def _():
        inbox[0, :, 0] = jnp.zeros_like(inbox[0, :, 0])
        inbox[0, :, 1] = jnp.zeros_like(inbox[0, :, 1])

    load.wait()
    for i in range(height):
        edge[0, i:i + 1, :] = e_v[i, PAD:PAD + 1, :]
        edge[1, i:i + 1, :] = e_v[i, PAD + width - 1:PAD + width, :]

    @pl.when(jnp.logical_not(has_down))
    def _():
        halo[0] = jnp.zeros_like(halo[0])

    @pl.when(jnp.logical_not(has_up))
    def _():
        halo[1] = jnp.zeros_like(halo[1])

    count = (
        jnp.where(p > 0, 1, 0) + jnp.where(p < gx_size - 1, 1, 0)
        + jnp.where(has_down, 1, 0) + jnp.where(has_up, 1, 0)
    )
    pl.semaphore_wait(barrier, count)

    def halo_copy(side, device):
        return pltpu.make_async_remote_copy(
            src_ref=edge.at[side], dst_ref=halo.at[1 - side],
            send_sem=halo_send.at[side], recv_sem=halo_recv.at[1 - side],
            device_id=device, device_id_type=MESH,
        )

    to_down = halo_copy(0, (p, q - 1))
    to_up = halo_copy(1, (p, q + 1))

    @pl.when(has_down)
    def _():
        to_down.start()

    @pl.when(has_up)
    def _():
        to_up.start()

    def wait_halo(k):
        if k == 0:
            @pl.when(has_down)
            def _():
                to_up.wait_recv()

            for i in range(height):
                e_v[i, PAD - 1:PAD, :] = halo[0, i:i + 1, :]
        if k == chunks - 1:
            @pl.when(has_up)
            def _():
                to_down.wait_recv()

            for i in range(height):
                e_v[i, PAD + width:PAD + width + 1, :] = halo[1, i:i + 1, :]

    def make_source(k):
        wait_halo(k)
        at = k * size

        def row(i, carry):
            here = e_v[i, PAD + at:PAD + at + size, :]
            before = e_v[i, PAD + at - 1:PAD + at + size - 1, :]
            after = e_v[i, PAD + at + 1:PAD + at + size + 1, :]
            b_v[i, at:at + size, :] = here + Y_WEIGHT * (before - 2.0 * here + after)
            return carry

        lax.fori_loop(0, height, row, 0, unroll=True)

    def message(k):
        return pltpu.make_async_remote_copy(
            src_ref=outbox.at[k], dst_ref=inbox.at[slot, k],
            send_sem=msg_send.at[k], recv_sem=msg_recv.at[slot, k],
            device_id=(inward, q), device_id_type=MESH,
        )

    def arrival(s, k):
        return pltpu.make_async_remote_copy(
            src_ref=outbox.at[k], dst_ref=inbox.at[s, k],
            send_sem=msg_send.at[k], recv_sem=msg_recv.at[s, k],
            device_id=(inward, q), device_id_type=MESH,
        )

    def reply(k):
        return pltpu.make_async_remote_copy(
            src_ref=usend.at[k], dst_ref=ubox.at[k],
            send_sem=u_send.at[k], recv_sem=u_recv.at[k],
            device_id=(outward, q), device_id_type=MESH,
        )

    def eliminate(k):
        rows = slice(k * size, (k + 1) * size)

        @pl.when(is_left)
        def _():
            e, f = inbox[0, k, 0], inbox[0, k, 1]
            c = c_v[0, rows, :]
            g = 1.0 / (c + e)
            r = c * g
            r_v[0, rows, :] = r
            g_v[0, rows, :] = g * f
            e = 1.0 + jnp.where(p == 0, c, r * e)
            f = b_v[0, rows, :] + r * f

            def step(i, carry):
                e, f = carry
                c = c_v[i, rows, :]
                g = 1.0 / (c + e)
                r = c * g
                r_v[i, rows, :] = r
                g_v[i, rows, :] = g * f
                return 1.0 + r * e, b_v[i, rows, :] + r * f

            e, f = lax.fori_loop(1, height, step, (e, f), unroll=True)
            outbox[k, 0] = e
            outbox[k, 1] = f

        @pl.when(is_right)
        def _():
            def step(t, carry):
                e, f = carry
                i = height - 1 - t
                e = 1.0 + e
                f = b_v[i, rows, :] + f
                c = c_v[i, rows, :]
                g = 1.0 / (c + e)
                r = c * g
                r_v[i, rows, :] = r
                g_v[i, rows, :] = g * f
                return r * e, r * f

            e, f = lax.fori_loop(0, height, step, (inbox[0, k, 0], inbox[0, k, 1]), unroll=True)
            outbox[k, 0] = e
            outbox[k, 1] = f

    def substitute(k):
        rows = slice(k * size, (k + 1) * size)

        @pl.when(is_left)
        def _():
            u = ubox[k]
            out_ref[height - 1, rows, :] = u

            def step(t, u):
                i = height - 1 - t
                u = g_v[i, rows, :] + r_v[i, rows, :] * u
                out_ref[i - 1, rows, :] = u
                return u

            u = lax.fori_loop(0, height - 1, step, u, unroll=True)
            usend[k] = g_v[0, rows, :] + r_v[0, rows, :] * u

        @pl.when(is_right)
        def _():
            def step(i, u):
                u = g_v[i, rows, :] + r_v[i, rows, :] * u
                out_ref[i, rows, :] = u
                return u

            usend[k] = lax.fori_loop(0, height, step, ubox[k], unroll=True)

    @pl.when(not_end)
    def _():
        for k in order:
            make_source(k)

    for step in range(chunks + lag):
        if step < chunks:
            k = order[step]
            face_load(k).wait()

            @pl.when(is_end)
            def _():
                make_source(k)

            @pl.when(not_end)
            def _():
                arrival(0, k).wait_recv()

            eliminate(k)
            message(k).start()
        if step >= lag:
            k = order[step - lag]

            @pl.when(is_mid)
            def _():
                arrival(1, k).wait_recv()
                ubox[k] = (outbox[k, 1] + inbox[1, k, 1]) / (outbox[k, 0] + inbox[1, k, 0])

            @pl.when(not_mid)
            def _():
                reply(k).wait_recv()

            substitute(k)

            @pl.when(not_end)
            def _():
                reply(k).start()

    for k in order:
        message(k).wait_send()

        @pl.when(not_end)
        def _():
            reply(k).wait_send()

    @pl.when(has_down)
    def _():
        to_down.wait_send()

    @pl.when(has_up)
    def _():
        to_up.wait_send()


def body(energy, coupling):
    height, width, depth = energy.shape
    gx_size, gy_size = lax.axis_size("gx"), lax.axis_size("gy")
    size = width // CHUNKS
    f32 = jnp.float32
    block = pltpu.VMEM((height, width, depth), f32)
    dma = pltpu.SemaphoreType.DMA
    return pl.pallas_call(
        functools.partial(kernel, gx_size, gy_size, CHUNKS, LAG),
        out_shape=jax.ShapeDtypeStruct(energy.shape, f32),
        in_specs=[pl.BlockSpec(memory_space=pl.ANY)] * 2,
        out_specs=pl.BlockSpec(memory_space=pltpu.VMEM),
        scratch_shapes=[
            pltpu.VMEM((height, width + 2 * PAD, depth), f32),
            block, block, block, block,
            pltpu.VMEM((2, height, depth), f32),
            pltpu.VMEM((2, height, depth), f32),
            pltpu.VMEM((CHUNKS, 2, size, depth), f32),
            pltpu.VMEM((2, CHUNKS, 2, size, depth), f32),
            pltpu.VMEM((CHUNKS, size, depth), f32),
            pltpu.VMEM((CHUNKS, size, depth), f32),
            dma, dma((CHUNKS,)), dma((2,)), dma((2,)),
            dma((CHUNKS,)), dma((2, CHUNKS)), dma((CHUNKS,)), dma((CHUNKS,)),
        ],
        compiler_params=pltpu.CompilerParams(
            collective_id=0, has_side_effects=True, vmem_limit_bytes=32 * 1024 * 1024
        ),
        cost_estimate=pl.CostEstimate(
            flops=30 * height * width * depth, bytes_accessed=12 * height * width * depth, transcendentals=0
        ),
    )(energy, coupling)


def solution(mesh):
    spec = P("gx", "gy", None)
    return jax.shard_map(body, mesh=mesh, in_specs=(spec, spec), out_specs=spec, check_vma=False)
```

time: 165 us -> 26.6 us (0.16); the launches traced: 162 us -> 26.4 us
  other arithmetic: 75.3 us -> 0 us
  waiting for transfers between devices: 40.9 us -> 0 us
  Pallas kernels: 0 us -> 22.9 us
  local copies, waits for them, and re-layouts: 23.2 us -> 3.42 us
  between operations: 13.6 us -> 0.01 us
  starting transfers between devices: 8.3 us -> 0 us
    dynamic_update_slice x57 -> x0, other arithmetic: 68.2 us -> none  [many_solve(): lax.scan(forward, start, (diag_part, lower_part, upper_part, sources))]
    all_gather x1 -> x0, waiting for transfers between devices: 31.1 us -> none  [body(): gathered = lax.all_gather(bundle, 'gx', axis=0, tiled=True)]
    pallas_call x0 -> x1, Pallas kernels: none -> 22.9 us  [body(): pl.pallas_call(functools.partial(kernel, gx_size, gy_size, CHUNKS, LAG),...]
    mul x15 -> x0, local copies, waits for them, and re-layouts: 12.7 us -> none  [backward(): result = value_row - ratio_row[None] * later_value]
    ppermute x4 -> x0, waiting for transfers between devices: 9.85 us -> none  [the longest x2 9.85 us: shifted(): lax.ppermute(value, axis, [(source, source + steps) for source in range(i...]
    ppermute x4 -> x0, starting transfers between devices: 8.3 us -> none  [the longest x2 4.65 us: shifted(): lax.ppermute(value, axis, [(source, source + steps) for source in range(i...]
    another operation x4 -> x0, other arithmetic: 4.65 us -> none  [the longest x2 3.92 us: body(): jnp.stack([source_term[:height - 1], left_source, right_source], 1)]
    another operation x6 -> x0, local copies, waits for them, and re-layouts: 4.12 us -> none
  transfers between devices with their start and end apart: 5 -> 0, of which waited for: 3 -> 0; matrix products, arithmetic and copies ran while one was open for 4% -> 0% of each run, Pallas kernels for 0% -> 0%
where the time goes in v1:
time: 26.6 us; the launch traced here: 26.4 us
  Pallas kernels  22.9 us (86%)
  local copies, waits for them, and re-layouts  3.42 us (13%)
    pallas_call x1, Pallas kernels, body(): pl.pallas_call(functools.partial(kernel, gx_size, gy_size, CHUNKS, LAG),...  22.9 us
    unnamed x5, local copies, waits for them, and re-layouts  3.42 us

profile of v1, /device:TPU:0, one launch (start us, length us, event | category | flops | bytes accessed | tf_op | source)
XLA Modules:
  0.0 26.4 jit_solution(2790065230170970506)
XLA Ops:
  0.0 0.0 copy-start
  0.0 1.2 %copy-done = f32[16,128,128]{2,1,0:T(8,128)S(1)} copy-done((f32[16,128,128]{2,1,0:T(8,128)S(1)}, f32[16,128,128]{2,1,0:T(8,128)}, u32[]{:S(2)}) %copy-start) | copy-done | bytes 1048600
  1.2 0.0 copy-start.1
  1.2 1.2 %copy-done.1 = f32[16,128,128]{2,1,0:T(8,128)S(1)} copy-done((f32[16,128,128]{2,1,0:T(8,128)S(1)}, f32[16,128,128]{2,1,0:T(8,128)}, u32[]{:S(2)}) %copy-start.1) | copy-done | bytes 1048600
  2.5 22.9 %shard_map.28 = f32[16,128,128]{2,1,0:T(8,128)S(1)} custom-call(f32[16,128,128]{2,1,0:T(8,128)S(1)} %copy-done, f32[16,128,128]{2,1,0:T(8,128)S(1)} %copy-done.1), custom_call_target="tpu_custom_call" | custom-call | flops 7864320 | bytes 3145728 | tf_op jit(solution)/shard_map/pallas_call | solution.py:285
  25.4 1.0 %copy.4 = f32[16,128,128]{2,1,0:T(8,128)} copy(f32[16,128,128]{2,1,0:T(8,128)S(1)} %shard_map.28) | data formatting | bytes 2097152
Async XLA Ops:
  0.0 1.2 %copy-start = (f32[16,128,128]{2,1,0:T(8,128)S(1)}, f32[16,128,128]{2,1,0:T(8,128)}, u32[]{:S(2)}) copy-start(f32[16,128,128]{2,1,0:T(8,128)} %energy_ref.1) | copy-start | bytes 3145732
  1.2 1.2 %copy-start.1 = (f32[16,128,128]{2,1,0:T(8,128)S(1)}, f32[16,128,128]{2,1,0:T(8,128)}, u32[]{:S(2)}) copy-start(f32[16,128,128]{2,1,0:T(8,128)} %coupling_ref.1) | copy-start | bytes 3145732

commit v2 on v1

v2 whole, which is shorter than its diff:
```python
import functools

import jax
import jax.numpy as jnp
from jax import lax
from jax.experimental import pallas as pl
from jax.experimental.pallas import tpu as pltpu
from jax.sharding import PartitionSpec as P

Y_WEIGHT = 0.15
PIECES = 4
PAD = 8
VMEM_LIMIT = 52 * 1024 * 1024
MESH = pl.DeviceIdType.MESH


def chunk_list(width):
    tiles = width // PAD - 2
    cuts = [2 * PAD + PAD * (tiles * n // PIECES) for n in range(PIECES + 1)]
    return [(a, b - a) for a, b in zip(cuts, cuts[1:])] + [(0, 2 * PAD)]


def kernel(
    gx_size, gy_size, energy_ref, coupling_ref, out_ref,
    e_v, c_v, b_v, r_v, g_v, edge, halo, outbox, inbox, usend, ubox,
    load_sem, face_sem, halo_send, halo_recv, msg_send, msg_recv, u_send, u_recv,
):
    height, width, _ = energy_ref.shape
    chunks = chunk_list(width)
    count = len(chunks)
    p, q = lax.axis_index("gx"), lax.axis_index("gy")
    half = gx_size // 2
    is_left = p < half
    is_right = p >= half
    is_end = (p == 0) | (p == gx_size - 1)
    is_mid = (p == half - 1) | (p == half)
    not_end = jnp.logical_not(is_end)
    not_mid = jnp.logical_not(is_mid)
    inward = jnp.where(is_left, p + 1, p - 1)
    outward = jnp.where(is_left, p - 1, p + 1)
    slot = jnp.where(is_mid, 1, 0)
    has_down, has_up = q > 0, q < gy_size - 1

    def segments(k):
        start, size = chunks[k]
        if start == 0:
            return [(0, width - PAD, PAD), (PAD, 0, PAD)]
        return [(0, start - PAD, size)]

    def take(ref, i, k, shift=0):
        parts = [ref[i, line + shift:line + shift + n, :] for _, line, n in segments(k)]
        return parts[0] if len(parts) == 1 else jnp.concatenate(parts, axis=0)

    def put(ref, i, k, value):
        for at, line, n in segments(k):
            ref[i, line:line + n, :] = value[at:at + n]

    def rows(k):
        start, size = chunks[k]
        return slice(start, start + size)

    barrier = pltpu.get_barrier_semaphore()

    def greet(cond, device):
        @pl.when(cond)
        def _():
            pl.semaphore_signal(barrier, inc=1, device_id=device, device_id_type=MESH)

    greet(p > 0, (p - 1, q))
    greet(p < gx_size - 1, (p + 1, q))
    greet(has_down, (p, q - 1))
    greet(has_up, (p, q + 1))

    load = pltpu.make_async_copy(energy_ref, e_v.at[:, PAD:PAD + width, :], load_sem)
    load.start()
    face_load = pltpu.make_async_copy(coupling_ref, c_v, face_sem)
    face_load.start()

    @pl.when(is_end)
    def _():
        inbox[0] = jnp.zeros_like(inbox[0])

    load.wait()
    for i in range(height):
        edge[0, i:i + 1, :] = e_v[i, PAD:PAD + 1, :]
        edge[1, i:i + 1, :] = e_v[i, PAD + width - 1:PAD + width, :]

    @pl.when(jnp.logical_not(has_down))
    def _():
        halo[0] = jnp.zeros_like(halo[0])

    @pl.when(jnp.logical_not(has_up))
    def _():
        halo[1] = jnp.zeros_like(halo[1])

    def halo_copy(side, device):
        return pltpu.make_async_remote_copy(
            src_ref=edge.at[side], dst_ref=halo.at[1 - side],
            send_sem=halo_send.at[side], recv_sem=halo_recv.at[1 - side],
            device_id=device, device_id_type=MESH,
        )

    to_down = halo_copy(0, (p, q - 1))
    to_up = halo_copy(1, (p, q + 1))

    def make_source(k):
        def row(i, carry):
            here, before, after = take(e_v, i, k, PAD), take(e_v, i, k, PAD - 1), take(e_v, i, k, PAD + 1)
            b_v[i, rows(k), :] = here + Y_WEIGHT * (before - 2.0 * here + after)
            return carry

        lax.fori_loop(0, height, row, 0, unroll=True)

    def message(s, k):
        return pltpu.make_async_remote_copy(
            src_ref=outbox.at[:, rows(k), :], dst_ref=inbox.at[s, :, rows(k), :],
            send_sem=msg_send.at[k], recv_sem=msg_recv.at[s, k],
            device_id=(inward, q), device_id_type=MESH,
        )

    def reply(k):
        return pltpu.make_async_remote_copy(
            src_ref=usend.at[rows(k)], dst_ref=ubox.at[rows(k)],
            send_sem=u_send.at[k], recv_sem=u_recv.at[k],
            device_id=(outward, q), device_id_type=MESH,
        )

    def eliminate(k):
        at = rows(k)

        @pl.when(is_left)
        def _():
            def step(i, carry):
                e, f = carry
                c = take(c_v, i, k)
                g = 1.0 / (c + e)
                r = c * g
                r_v[i, at, :] = r
                g_v[i, at, :] = g * f
                through = r * e
                if isinstance(i, int):
                    through = jnp.where(p == 0, c, through)
                return 1.0 + through, b_v[i, at, :] + r * f

            carry = step(0, (inbox[0, 0, at, :], inbox[0, 1, at, :]))
            e, f = lax.fori_loop(1, height, step, carry, unroll=True)
            outbox[0, at, :] = e
            outbox[1, at, :] = f

        @pl.when(is_right)
        def _():
            def step(t, carry):
                e, f = carry
                i = height - 1 - t
                e = 1.0 + e
                f = b_v[i, at, :] + f
                c = take(c_v, i, k)
                g = 1.0 / (c + e)
                r = c * g
                r_v[i, at, :] = r
                g_v[i, at, :] = g * f
                return r * e, r * f

            carry = (inbox[0, 0, at, :], inbox[0, 1, at, :])
            e, f = lax.fori_loop(0, height, step, carry, unroll=True)
            outbox[0, at, :] = e
            outbox[1, at, :] = f

    def prepare(k):
        at = rows(k)

        def step(t, carry):
            a, b = carry
            i = jnp.where(is_left, height - 1 - t, t)
            r = r_v[i, at, :]
            a = g_v[i, at, :] + r * a
            b = r * b
            g_v[i, at, :] = a
            r_v[i, at, :] = b
            return a, b

        first = jnp.where(is_left, height - 1, 0)
        lax.fori_loop(1, height, step, (g_v[first, at, :], r_v[first, at, :]), unroll=True)

    def substitute(k):
        at = rows(k)

        @pl.when(is_left)
        def _():
            u = ubox[at, :]
            put(out_ref, height - 1, k, u)

            def step(i, carry):
                put(out_ref, i - 1, k, g_v[i, at, :] + r_v[i, at, :] * u)
                return carry

            lax.fori_loop(1, height, step, 0, unroll=True)

        @pl.when(is_right)
        def _():
            u = ubox[at, :]

            def step(i, carry):
                put(out_ref, i, k, g_v[i, at, :] + r_v[i, at, :] * u)
                return carry

            lax.fori_loop(0, height, step, 0, unroll=True)

    for k in range(count - 1):
        make_source(k)
    face_load.wait()
    greeted = (
        jnp.where(p > 0, 1, 0) + jnp.where(p < gx_size - 1, 1, 0)
        + jnp.where(has_down, 1, 0) + jnp.where(has_up, 1, 0)
    )

    @pl.when(is_end)
    def _():
        eliminate(0)

    pl.semaphore_wait(barrier, greeted)

    @pl.when(has_down)
    def _():
        to_down.start()

    @pl.when(has_up)
    def _():
        to_up.start()

    for k in range(count):
        if k == count - 1:
            @pl.when(has_down)
            def _():
                to_up.wait_recv()

            @pl.when(has_up)
            def _():
                to_down.wait_recv()

            for i in range(height):
                e_v[i, PAD - 1:PAD, :] = halo[0, i:i + 1, :]
                e_v[i, PAD + width:PAD + width + 1, :] = halo[1, i:i + 1, :]
            make_source(k)

        @pl.when(not_end)
        def _():
            message(0, k).wait_recv()
            if k == 0:
                eliminate(k)

        if k > 0:
            eliminate(k)
        message(slot, k).start()
        prepare(k)

    last = jnp.where(is_left, 0, height - 1)
    for k in range(count):
        at = rows(k)

        @pl.when(is_mid)
        def _():
            message(1, k).wait_recv()
            ubox[at, :] = (outbox[1, at, :] + inbox[1, 1, at, :]) / (outbox[0, at, :] + inbox[1, 0, at, :])

        @pl.when(not_mid)
        def _():
            reply(k).wait_recv()

        @pl.when(not_end)
        def _():
            usend[at, :] = g_v[last, at, :] + r_v[last, at, :] * ubox[at, :]
            reply(k).start()

        substitute(k)

    for k in range(count):
        message(slot, k).wait_send()

        @pl.when(not_end)
        def _():
            reply(k).wait_send()

    @pl.when(has_down)
    def _():
        to_down.wait_send()

    @pl.when(has_up)
    def _():
        to_up.wait_send()


def body(energy, coupling):
    height, width, depth = energy.shape
    gx_size, gy_size = lax.axis_size("gx"), lax.axis_size("gy")
    count = len(chunk_list(width))
    f32 = jnp.float32
    block = pltpu.VMEM((height, width, depth), f32)
    plane = pltpu.VMEM((width, depth), f32)
    dma = pltpu.SemaphoreType.DMA
    return pl.pallas_call(
        functools.partial(kernel, gx_size, gy_size),
        out_shape=jax.ShapeDtypeStruct(energy.shape, f32),
        in_specs=[pl.BlockSpec(memory_space=pl.ANY)] * 2,
        out_specs=pl.BlockSpec(memory_space=pltpu.VMEM),
        scratch_shapes=[
            pltpu.VMEM((height, width + 2 * PAD, depth), f32),
            block, block, block, block,
            pltpu.VMEM((2, height, depth), f32),
            pltpu.VMEM((2, height, depth), f32),
            pltpu.VMEM((2, width, depth), f32),
            pltpu.VMEM((2, 2, width, depth), f32),
            plane, plane,
            dma, dma, dma((2,)), dma((2,)),
            dma((count,)), dma((2, count)), dma((count,)), dma((count,)),
        ],
        compiler_params=pltpu.CompilerParams(
            collective_id=0, has_side_effects=True, vmem_limit_bytes=VMEM_LIMIT
        ),
        cost_estimate=pl.CostEstimate(
            flops=30 * height * width * depth, bytes_accessed=12 * height * width * depth, transcendentals=0
        ),
    )(energy, coupling)


def solution(mesh):
    spec = P("gx", "gy", None)
    return jax.shard_map(body, mesh=mesh, in_specs=(spec, spec), out_specs=spec, check_vma=False)
```

time: 26.6 us -> 16.5 us (0.62)
  Pallas kernels: 22.9 us -> 15.3 us
  local copies, waits for them, and re-layouts: 3.42 us -> 0.97 us
    pallas_call x1, Pallas kernels: 22.9 us -> 15.3 us  [body(): pl.pallas_call(functools.partial(kernel, gx_size, gy_size), out_shape=jax...]
    unnamed x5 -> x1, local copies, waits for them, and re-layouts: 3.42 us -> 0.97 us
where the time goes in v2:
time: 16.5 us; the launch traced here: 16.3 us
  Pallas kernels  15.3 us (93%)
  local copies, waits for them, and re-layouts  0.97 us (6%)
    pallas_call x1, Pallas kernels, body(): pl.pallas_call(functools.partial(kernel, gx_size, gy_size), out_shape=jax...  15.3 us
    unnamed x1, local copies, waits for them, and re-layouts  0.97 us

profile of v2, /device:TPU:0, one launch (start us, length us, event | category | flops | bytes accessed | tf_op | source)
XLA Modules:
  0.0 16.3 jit_solution(8844843063315091946)
XLA Ops:
  0.0 15.3 %shard_map.28 = f32[16,128,128]{2,1,0:T(8,128)S(1)} custom-call(f32[16,128,128]{2,1,0:T(8,128)} %energy_ref.1, f32[16,128,128]{2,1,0:T(8,128)} %coupling_ref.1), custom_call_target="tpu_custom_call" | custom-call | flops 7864320 | bytes 3145728 | tf_op jit(solution)/shard_map/pallas_call | solution.py:301
  15.3 1.0 %copy.4 = f32[16,128,128]{2,1,0:T(8,128)} copy(f32[16,128,128]{2,1,0:T(8,128)S(1)} %shard_map.28) | data formatting | bytes 2097152

commit v3 on v2

--- a/solution.py
+++ b/solution.py
@@ -8,7 +8,7 @@
 from jax.sharding import PartitionSpec as P
 
 Y_WEIGHT = 0.15
-PIECES = 4
+PIECES = 7
 PAD = 8
 VMEM_LIMIT = 52 * 1024 * 1024
 MESH = pl.DeviceIdType.MESH
@@ -133,7 +133,7 @@
             def step(i, carry):
                 e, f = carry
                 c = take(c_v, i, k)
-                g = 1.0 / (c + e)
+                g = pl.reciprocal(c + e)
                 r = c * g
                 r_v[i, at, :] = r
                 g_v[i, at, :] = g * f
@@ -155,7 +155,7 @@
                 e = 1.0 + e
                 f = b_v[i, at, :] + f
                 c = take(c_v, i, k)
-                g = 1.0 / (c + e)
+                g = pl.reciprocal(c + e)
                 r = c * g
                 r_v[i, at, :] = r
                 g_v[i, at, :] = g * f
@@ -252,6 +252,8 @@
         if k > 0:
             eliminate(k)
         message(slot, k).start()
+
+    for k in range(count):
         prepare(k)
 
     last = jnp.where(is_left, 0, height - 1)

time: 16.5 us -> 16.2 us (0.982)
  Pallas kernels: 15.3 us -> 15.1 us
    pallas_call x1, Pallas kernels: 15.3 us -> 15.1 us  [body(): pl.pallas_call(functools.partial(kernel, gx_size, gy_size), out_shape=jax...]
where the time goes in v3:
time: 16.2 us; the launch traced here: 16.1 us
  Pallas kernels  15.1 us (93%)
  local copies, waits for them, and re-layouts  0.97 us (6%)
    pallas_call x1, Pallas kernels, body(): pl.pallas_call(functools.partial(kernel, gx_size, gy_size), out_shape=jax...  15.1 us
    unnamed x1, local copies, waits for them, and re-layouts  0.97 us

profile of v3, /device:TPU:0, one launch (start us, length us, event | category | flops | bytes accessed | tf_op | source)
XLA Modules:
  0.0 16.1 jit_solution(618593984531221864)
XLA Ops:
  0.0 15.1 %shard_map.28 = f32[16,128,128]{2,1,0:T(8,128)S(1)} custom-call(f32[16,128,128]{2,1,0:T(8,128)} %energy_ref.1, f32[16,128,128]{2,1,0:T(8,128)} %coupling_ref.1), custom_call_target="tpu_custom_call" | custom-call | flops 7864320 | bytes 3145728 | tf_op jit(solution)/shard_map/pallas_call | solution.py:303
  15.1 1.0 %copy.4 = f32[16,128,128]{2,1,0:T(8,128)} copy(f32[16,128,128]{2,1,0:T(8,128)S(1)} %shard_map.28) | data formatting | bytes 2097152

commit v4 on v3

--- a/solution.py
+++ b/solution.py
@@ -274,7 +274,14 @@
             usend[at, :] = g_v[last, at, :] + r_v[last, at, :] * ubox[at, :]
             reply(k).start()
 
-        substitute(k)
+        @pl.when(not_mid)
+        def _():
+            substitute(k)
+
+    @pl.when(is_mid)
+    def _():
+        for k in range(count):
+            substitute(k)
 
     for k in range(count):
         message(slot, k).wait_send()

time: 16.2 us -> 16.2 us (level)
  no operation moved by 1% of the time
where the time goes in v4:
time: 16.2 us; the launch traced here: 16.1 us
  Pallas kernels  15.1 us (93%)
  local copies, waits for them, and re-layouts  0.97 us (6%)
    pallas_call x1, Pallas kernels, body(): pl.pallas_call(functools.partial(kernel, gx_size, gy_size), out_shape=jax...  15.1 us
    unnamed x1, local copies, waits for them, and re-layouts  0.97 us

profile of v4, /device:TPU:0, one launch (start us, length us, event | category | flops | bytes accessed | tf_op | source)
XLA Modules:
  0.0 16.1 jit_solution(16618654413368071537)
XLA Ops:
  0.0 15.1 %shard_map.28 = f32[16,128,128]{2,1,0:T(8,128)S(1)} custom-call(f32[16,128,128]{2,1,0:T(8,128)} %energy_ref.1, f32[16,128,128]{2,1,0:T(8,128)} %coupling_ref.1), custom_call_target="tpu_custom_call" | custom-call | flops 7864320 | bytes 3145728 | tf_op jit(solution)/shard_map/pallas_call | solution.py:310
  15.1 1.0 %copy.4 = f32[16,128,128]{2,1,0:T(8,128)} copy(f32[16,128,128]{2,1,0:T(8,128)S(1)} %shard_map.28) | data formatting | bytes 2097152
